TPU v7x, 512 devices: a whole 4x8x8 slice. The times are simulated.
512 devices in a mesh: dp: 64 (over y_lo, x, z), space: 8 (over y_hi, core).
Axes of the slice: x: 4, y: 8 (y_hi: 4, y_lo: 2; y = y_hi * 2 + y_lo), z: 8, core: 2. Of those that a mesh axis runs over, the one named last changes fastest.
Arguments:
- field_in: bfloat16 [1, 512, 512, 128], P(None, 'space', 'dp'), may hold values from -6 to 6
- pre_act: bfloat16 [1, 512, 512, 128], P(None, 'space', 'dp'), may hold values from -8 to 8
- cotangent: bfloat16 [1, 512, 512, 128], P(None, 'space', 'dp'), may hold values from -6 to 6
- spec_weight: bfloat16 [64, 64, 2, 128, 128], P('dp', 'space'), may hold values from -0.25 to 0.25
- local_weight: bfloat16 [128, 128], replicated, may hold values from -0.5 to 0.5
Outputs:
- grad_input: bfloat16 [1, 512, 512, 128], P(None, 'space', 'dp')
- grad_spectral: bfloat16 [64, 64, 2, 128, 128], P('dp', 'space')
- grad_local: float32 [128, 128], replicated
- grad_bias: float32 [128], replicated
All inputs are finite; a program needn't handle non-finite values.
Results may differ from a plain program's by a relative error of at most 0.0075.
The roundings to bfloat16 on the way count: a program that leaves them out, or rounds other values in their place, can miss the bound.
Values may be sent and summed in bfloat16 or wider, within the bound.
A program may use at most 64 MiB of HBM per device.

v0:
```python
import math
import jax
import jax.numpy as jnp
from jax import lax
from jax.sharding import PartitionSpec as P

root_two_pi = 0.7978845608028654
cubic_coef = 0.044715


def gelu_slope(values):
    tangent = jnp.tanh(root_two_pi * (values + cubic_coef * values * values * values))
    return 0.5 * (1.0 + tangent) + 0.5 * values * (1.0 - tangent * tangent) * root_two_pi * (
        1.0 + 3.0 * cubic_coef * values * values
    )


def y_basis(grid_cols, ky_count):
    positions = jnp.arange(grid_cols, dtype=jnp.int32)
    frequency = jnp.arange(ky_count, dtype=jnp.int32)
    phases = positions[:, None] * frequency[None, :] % grid_cols
    angles = phases.astype(jnp.float32) * (2.0 * math.pi / grid_cols)
    basis_table = jnp.stack([jnp.cos(angles), -jnp.sin(angles)], axis=2).reshape(
        grid_cols, 2 * ky_count
    )
    return basis_table.astype(jnp.bfloat16)


def x_rows_table(positions, grid_rows, kx_count):
    mode_index = jnp.arange(kx_count, dtype=jnp.int32)
    frequency = jnp.where(mode_index < kx_count // 2, mode_index, mode_index - kx_count)
    phases = frequency[:, None] * positions[None, :] % grid_rows
    angles = phases.astype(jnp.float32) * (2.0 * math.pi / grid_rows)
    cosine = jnp.cos(angles)
    sine = jnp.sin(angles)
    upper_rows = jnp.stack([cosine, sine], axis=1)
    lower_rows = jnp.stack([-sine, cosine], axis=1)
    return jnp.stack([upper_rows, lower_rows], axis=0).astype(jnp.bfloat16)


def on_device(field_in, pre_act, cotangent, spec_weight, local_weight):
    batch_size, slab_rows, col_block, channels = field_in.shape
    space_count = lax.axis_size("space")
    data_count = lax.axis_size("dp")
    grid_rows = slab_rows * space_count
    grid_cols = col_block * data_count
    row_count = slab_rows // data_count
    held_count = space_count * row_count
    kx_local = spec_weight.shape[0]
    kx_count = kx_local * data_count
    ky_local = spec_weight.shape[1]
    ky_count = ky_local * space_count
    data_index = lax.axis_index("dp")
    space_index = lax.axis_index("space")
    y_table = y_basis(grid_cols, ky_count)
    held_rows = (
        jnp.arange(space_count, dtype=jnp.int32)[:, None] * slab_rows
        + data_index * row_count
        + jnp.arange(row_count, dtype=jnp.int32)[None, :]
    ).reshape(held_count)
    x_held = x_rows_table(held_rows, grid_rows, kx_count)
    delta_field = (cotangent.astype(jnp.float32) * gelu_slope(pre_act.astype(jnp.float32))).astype(
        jnp.bfloat16
    )
    local_term = jnp.einsum(
        "bxyc,bxyo->co", field_in, delta_field, preferred_element_type=jnp.float32
    )
    bias_term = jnp.sum(delta_field, axis=(0, 1, 2), dtype=jnp.float32)
    local_sum, bias_sum = lax.psum((local_term, bias_term), ("dp", "space"))
    stacked = jnp.stack([field_in, delta_field])
    lines = lax.all_to_all(stacked, "dp", split_axis=2, concat_axis=3, tiled=True)
    pairs = lax.all_to_all(
        jnp.einsum("fbxyc,yr->fbxrc", lines, y_table, preferred_element_type=jnp.float32).astype(
            jnp.bfloat16
        ),
        "space",
        split_axis=3,
        concat_axis=2,
        tiled=True,
    )
    field_count = pairs.shape[0]
    split_pairs = pairs.reshape(field_count, batch_size, held_count, ky_local, 2, channels)
    table = x_held
    owned = lax.psum_scatter(
        jnp.einsum("qjpx,fbxkpc->jfbkqc", table, split_pairs, preferred_element_type=jnp.float32),
        "dp",
        scatter_dimension=0,
        tiled=True,
    ).astype(jnp.bfloat16)
    input_owned = owned[:, 0]
    delta_owned = owned[:, 1]
    ky_index = space_index * ky_local + jnp.arange(ky_local, dtype=jnp.int32)
    ky_scale = jnp.where(ky_index == 0, 1.0, 2.0).astype(jnp.float32) / (grid_rows * grid_cols)
    products = jnp.einsum(
        "jbkqc,jbkpo->jkqpco", input_owned, delta_owned, preferred_element_type=jnp.float32
    )
    grad_real = products[:, :, 0, 0] + products[:, :, 1, 1]
    grad_imag = products[:, :, 0, 1] - products[:, :, 1, 0]
    grad_spectral = (
        jnp.stack([grad_real, grad_imag], axis=2)
        * (ky_scale / batch_size)[None, :, None, None, None]
    ).astype(jnp.bfloat16)
    adjoint = jnp.einsum(
        "jbkpo,jkqco->bjkpqc", delta_owned, spec_weight, preferred_element_type=jnp.float32
    )
    back_real = adjoint[:, :, :, 0, 0] + adjoint[:, :, :, 1, 1]
    back_imag = adjoint[:, :, :, 1, 0] - adjoint[:, :, :, 0, 1]
    mode_back = (
        jnp.stack([back_real, back_imag], axis=3) * ky_scale[None, None, :, None, None]
    ).astype(jnp.bfloat16)
    table = x_held
    along_x = jnp.einsum(
        "qjpx,bjkqc->bxkpc",
        table,
        lax.all_gather(mode_back, "dp", axis=1, tiled=True),
        preferred_element_type=jnp.float32,
    ).astype(jnp.bfloat16)
    along_x = along_x.reshape(batch_size, held_count, 2 * ky_local, channels)
    lines_back = lax.all_to_all(along_x, "space", split_axis=1, concat_axis=2, tiled=True)
    local_part = jnp.einsum(
        "bxyo,co->bxyc", delta_field, local_weight, preferred_element_type=jnp.float32
    )
    slab_lines = lax.all_gather(lines_back, "dp", axis=1, tiled=True)
    y_block = lax.dynamic_slice_in_dim(y_table, data_index * col_block, col_block, 0)
    spectral_part = jnp.einsum(
        "bxrc,yr->bxyc", slab_lines, y_block, preferred_element_type=jnp.float32
    ).astype(jnp.bfloat16)
    grad_input = (spectral_part.astype(jnp.float32) + local_part).astype(jnp.bfloat16)
    return (grad_input, grad_spectral, local_sum / batch_size, bias_sum / batch_size)


def solution(mesh):
    placed = (
        P(None, "space", "dp", None),
        P(None, "space", "dp", None),
        P(None, "space", "dp", None),
        P("dp", "space", None, None, None),
        P(),
    )
    return jax.shard_map(
        on_device,
        mesh=mesh,
        in_specs=placed,
        out_specs=(P(None, "space", "dp", None), P("dp", "space", None, None, None), P(), P()),
        check_vma=False,
    )
```

profile of v0, /device:TPU:16, one launch (start us, length us, event | category | flops | bytes accessed | tf_op | source)
XLA Modules:
  0.0 838.3 jit_solution(12355432250104961929)
XLA Ops:
  8.0 1.2 convert_reduce_fusion
  9.3 1.6 pad_maximum_fusion
  10.9 14.8 %all-to-all-start = ((bf16[2,1,64,8,128]{4,3,1,0,2:T(8,128)(2,1)}), bf16[2,1,64,8,128]{4,3,1,0,2:T(8,128)(2,1)S(1)}, u32[]{:S(2)}, u32[]{:S(2)}) async-start(bf16[2,1,64,8,128]{4,3,1,0,2:T(8,128)(2,1)} %pad_maximum_fusion), calls=%async_computation | async-start | bytes 524288 | tf_op jit(solution)/shard_map/all_to_all | solution.py:71
  25.7 0.5 sine_negate_fusion
  26.3 0.1 copy.82
  26.5 12.6 %all-to-all-done = bf16[2,1,64,8,128]{4,3,1,0,2:T(8,128)(2,1)S(1)} async-done(((bf16[2,1,64,8,128]{4,3,1,0,2:T(8,128)(2,1)}), bf16[2,1,64,8,128]{4,3,1,0,2:T(8,128)(2,1)S(1)}, u32[]{:S(2)}, u32[]{:S(2)}) %all-to-all-start) | async-done | bytes 262176 | tf_op jit(solution)/shard_map/all_to_all | solution.py:71
  39.2 0.2 fusion.16
  39.3 0.7 copy.85
  40.0 6.5 all-to-all-start.1
  46.6 0.1 fusion.59
  46.7 5.5 all-to-all-done.1
  52.3 0.3 convolution_bitcast_fusion
  52.6 1.6 copy.88
  54.2 311.5 %reduce-scatter.2.cloned.1.call-done = f32[1,2,1,8,2,128]{5,3,4,2,1,0:T(8,128)} async-done(((f32[64,2,1,8,2,128]{5,3,4,2,1,0:T(8,128)}), f32[1,2,1,8,2,128]{5,3,4,2,1,0:T(8,128)}) %reduce-scatter.2.cloned.1.call-update) | async-done | bytes 16400 | tf_op jit(solution)/shard_map/reduce_scatter | solution.py:84
  365.7 0.7 convert_element_type.130
  366.4 0.2 convolution_bitcast_fusion.4
  366.8 152.5 %all_gather.6 = bf16[1,64,8,2,128]{4,2,3,0,1:T(8,128)(2,1)S(1)} all-gather(bf16[1,1,8,2,128]{4,2,3,0,1:T(8,128)(2,1)S(1)} %fusion.55), channel_id=1, replica_groups=mesh['dp'=64,'space'=8] {'dp'}, dimensions={1}, use_global_device_ids=true | all-gather | bytes 266240 | tf_op jit(solution)/shard_map/all_gather | solution.py:115
  519.3 0.2 fusion.17
  519.5 0.6 copy.95
  520.1 6.3 all-to-all-start.2
  526.4 0.9 convolution_bitcast_fusion.2
  527.3 4.5 all-to-all-done.2
  531.9 0.6 copy-done.1
  532.6 96.2 %psum.15 = f32[128]{0:T(128)} all-reduce(f32[128]{0:T(128)S(1)} %get-tuple-element.28), channel_id=1, replica_groups=mesh['dp'=64,'space'=8] {'dp','space'}, use_global_device_ids=true, to_apply=%region_3.4 | all-reduce | flops 128 | bytes 1024 | tf_op jit(solution)/shard_map/psum | solution.py:69
  628.8 162.3 %all-reduce.2.cloned.1.call-done = f32[128,128]{0,1:T(8,128)} async-done(((f32[128,128]{0,1:T(8,128)}), f32[128,128]{0,1:T(8,128)}) %all-reduce.2.cloned.1.call-update) | async-done | bytes 65552 | tf_op jit(solution)/shard_map/psum | solution.py:69
  791.1 1.6 copy.98
  792.7 0.4 multiply_bitcast_fusion
  793.1 0.1 fusion.20
  793.2 1.0 fusion.18
  794.2 33.7 %all-gather.2.cloned.1.call-done = bf16[1,64,128,128]{3,2,0,1:T(8,128)(2,1)} async-done(((bf16[1,1,128,128]{3,2,0,1:T(8,128)(2,1)}), bf16[1,64,128,128]{3,2,0,1:T(8,128)(2,1)}) %all-gather.2.cloned.1.call-update) | async-done | bytes 2097168 | tf_op jit(solution)/shard_map/all_gather | solution.py:123
  827.9 2.1 fusion.13
  830.0 0.9 fusion.3
  (24 shorter events, 0.4 us)
Async XLA Ops:
  8.0 358.4 %copy-start = (bf16[1,8,2,128,128]{4,3,2,1,0:T(8,128)(2,1)S(1)}, bf16[1,8,2,128,128]{4,3,2,1,0:T(8,128)(2,1)}, u32[]{:S(2)}) copy-start(bf16[1,8,2,128,128]{4,3,2,1,0:T(8,128)(2,1)} %param.8) | copy-start | bytes 1572868
  10.9 28.2 %all-to-all-start = ((bf16[2,1,64,8,128]{4,3,1,0,2:T(8,128)(2,1)}), bf16[2,1,64,8,128]{4,3,1,0,2:T(8,128)(2,1)S(1)}, u32[]{:S(2)}, u32[]{:S(2)}) async-start(bf16[2,1,64,8,128]{4,3,1,0,2:T(8,128)(2,1)} %pad_maximum_fusion), calls=%async_computation | async-start | bytes 524288 | tf_op jit(solution)/shard_map/all_to_all | solution.py:71
  40.0 12.2 %all-to-all-start.1 = ((bf16[2,1,1,128,128]{4,0,2,1,3:T(2,128)(2,1)}), bf16[2,1,1,128,128]{4,0,2,1,3:T(2,128)(2,1)S(1)}, u32[]{:S(2)}, u32[]{:S(2)}) async-start(bf16[2,1,1,128,128]{4,0,2,1,3:T(2,128)(2,1)} %copy.85), calls=%async_computation.1 | async-start | bytes 131072 | tf_op jit(solution)/shard_map/all_to_all | solution.py:72
  46.6 319.1 %reduce-scatter.2.cloned.1.call-start = ((), (), s32[]{:S(2)}) async-start(), calls=%async_computation.4 | async-start | bytes 1064960 | tf_op jit(solution)/shard_map/reduce_scatter | solution.py:84
  52.6 473.8 %copy-start.2 = (bf16[1,64,8,128]{3,2,1,0:T(8,128)(2,1)S(1)}, bf16[1,64,8,128]{3,2,1,0:T(8,128)(2,1)}, u32[]{:S(2)}) copy-start(bf16[1,64,8,128]{3,2,1,0:T(8,128)(2,1)} %param.5) | copy-start | bytes 393220
  520.1 11.8 %all-to-all-start.2 = ((bf16[1,8,16,128]{3,2,0,1:T(8,128)(2,1)}), bf16[1,8,16,128]{3,2,0,1:T(8,128)(2,1)S(1)}, u32[]{:S(2)}, u32[]{:S(2)}) async-start(bf16[1,8,16,128]{3,2,0,1:T(8,128)(2,1)} %copy.95), calls=%async_computation.3 | async-start | bytes 65536 | tf_op jit(solution)/shard_map/all_to_all | solution.py:119
  526.4 264.7 %all-reduce.2.cloned.1.call-start = ((), (), s32[]{:S(2)}) async-start(), calls=%async_computation.6 | async-start | bytes 131072 | tf_op jit(solution)/shard_map/psum | solution.py:69
  527.3 300.6 %all-gather.2.cloned.1.call-start = ((), (), s32[]{:S(2)}) async-start(), calls=%async_computation.5 | async-start | bytes 2129920 | tf_op jit(solution)/shard_map/all_gather | solution.py:123
  531.9 0.6 copy-start.1
  793.2 36.8 %copy-start.3 = (bf16[128,128]{1,0:T(8,128)(2,1)S(1)}, bf16[128,128]{1,0:T(8,128)(2,1)}, u32[]{:S(2)}) copy-start(bf16[128,128]{1,0:T(8,128)(2,1)} %param.9) | copy-start | bytes 98308
Sparse Core Ops, SparseCore 0:
  54.4 311.3 reduce-scatter.1
  532.6 295.2 all-gather.1
Sparse Core Ops, SparseCore 1:
  533.2 257.9 all-reduce.1
where the time goes:
time: 839 us; the launch traced here: 838 us
  waiting for transfers between devices  530 us (63%)
  blocking collectives  249 us (30%)
  starting transfers between devices  27.7 us (3%)
  between operations  15.6 us (2%)
    reduce_scatter x1, waiting for transfers between devices, on_device(): lax.psum_scatter(jnp.einsum('qjpx,fbxkpc->jfbkqc', table, split_pairs, pr...  311 us
    psum x1, waiting for transfers between devices, on_device(): local_sum, bias_sum = lax.psum((local_term, bias_term), ('dp', 'space'))  162 us
    all_gather x1, blocking collectives, on_device(): lax.all_gather(mode_back, 'dp', axis=1, tiled=True)  152 us
    psum x1, blocking collectives, on_device(): local_sum, bias_sum = lax.psum((local_term, bias_term), ('dp', 'space'))  96.2 us
    all_gather x1, waiting for transfers between devices, on_device(): slab_lines = lax.all_gather(lines_back, 'dp', axis=1, tiled=True)  33.7 us
  transfers between devices with their start and end apart: 6, of which 6 were waited for; matrix products, arithmetic and copies ran while one was open for 1% of the time, Pallas kernels for 0%

commit v1 on v0

--- a/solution.py
+++ b/solution.py
@@ -112,7 +112,9 @@
     along_x = jnp.einsum(
         "qjpx,bjkqc->bxkpc",
         table,
-        lax.all_gather(mode_back, "dp", axis=1, tiled=True),
+        jnp.concatenate(
+            lax.all_to_all(jnp.stack([mode_back] * lax.axis_size("dp")), "dp", 0, 0), axis=1
+        ),
         preferred_element_type=jnp.float32,
     ).astype(jnp.bfloat16)
     along_x = along_x.reshape(batch_size, held_count, 2 * ky_local, channels)

time: 839 us -> 703 us (0.84)
  blocking collectives: 249 us -> 111 us
    all_gather x1 -> x0, blocking collectives: 152 us -> none  [on_device(): lax.all_gather(mode_back, 'dp', axis=1, tiled=True)]
    all_to_all x0 -> x1, blocking collectives: none -> 15.9 us  [on_device(): lax.all_to_all(jnp.stack([mode_back] * lax.axis_size('dp')), 'dp', 0, 0)]
where the time goes in v1:
time: 703 us; the launch traced here: 702 us
  waiting for transfers between devices  532 us (76%)
  blocking collectives  111 us (16%)
  starting transfers between devices  27.7 us (4%)
  between operations  15.6 us (2%)
    reduce_scatter x1, waiting for transfers between devices, on_device(): lax.psum_scatter(jnp.einsum('qjpx,fbxkpc->jfbkqc', table, split_pairs, pr...  311 us
    psum x1, waiting for transfers between devices, on_device(): local_sum, bias_sum = lax.psum((local_term, bias_term), ('dp', 'space'))  164 us
    psum x1, blocking collectives, on_device(): local_sum, bias_sum = lax.psum((local_term, bias_term), ('dp', 'space'))  95.4 us
    all_gather x1, waiting for transfers between devices, on_device(): slab_lines = lax.all_gather(lines_back, 'dp', axis=1, tiled=True)  33.7 us
    all_to_all x1, blocking collectives, on_device(): lax.all_to_all(jnp.stack([mode_back] * lax.axis_size('dp')), 'dp', 0, 0)  15.9 us
    all_to_all x1, starting transfers between devices, on_device(): lax.all_to_all(stacked, 'dp', split_axis=2, concat_axis=3, tiled=True)  14.8 us
  transfers between devices with their start and end apart: 6, of which 6 were waited for; matrix products, arithmetic and copies ran while one was open for 1% of the time, Pallas kernels for 0%

profile of v1, /device:TPU:16, one launch (start us, length us, event | category | flops | bytes accessed | tf_op | source)
XLA Modules:
  0.0 702.5 jit_solution(92217505039615164)
XLA Ops:
  8.0 1.2 convert_reduce_fusion
  9.3 1.6 pad_maximum_fusion
  10.9 14.8 %all-to-all-start = ((bf16[2,1,64,8,128]{4,3,1,0,2:T(8,128)(2,1)}), bf16[2,1,64,8,128]{4,3,1,0,2:T(8,128)(2,1)S(1)}, u32[]{:S(2)}, u32[]{:S(2)}) async-start(bf16[2,1,64,8,128]{4,3,1,0,2:T(8,128)(2,1)} %pad_maximum_fusion), calls=%async_computation | async-start | bytes 524288 | tf_op jit(solution)/shard_map/all_to_all | solution.py:71
  25.7 0.5 sine_negate_fusion
  26.3 0.1 copy.82
  26.5 12.6 %all-to-all-done = bf16[2,1,64,8,128]{4,3,1,0,2:T(8,128)(2,1)S(1)} async-done(((bf16[2,1,64,8,128]{4,3,1,0,2:T(8,128)(2,1)}), bf16[2,1,64,8,128]{4,3,1,0,2:T(8,128)(2,1)S(1)}, u32[]{:S(2)}, u32[]{:S(2)}) %all-to-all-start) | async-done | bytes 262176 | tf_op jit(solution)/shard_map/all_to_all | solution.py:71
  39.2 0.2 fusion.16
  39.3 0.7 copy.85
  40.0 6.5 all-to-all-start.1
  46.7 5.5 all-to-all-done.1
  52.3 0.3 convolution_bitcast_fusion
  52.6 1.6 copy.88
  54.2 311.5 %reduce-scatter.2.cloned.1.call-done = f32[1,2,1,8,2,128]{5,3,4,2,1,0:T(8,128)} async-done(((f32[64,2,1,8,2,128]{5,3,4,2,1,0:T(8,128)}), f32[1,2,1,8,2,128]{5,3,4,2,1,0:T(8,128)}) %reduce-scatter.2.cloned.1.call-update) | async-done | bytes 16400 | tf_op jit(solution)/shard_map/reduce_scatter | solution.py:84
  365.7 0.7 convert_element_type.129
  366.4 0.2 convolution_bitcast_fusion.4
  366.8 0.1 stack.43
  366.9 15.9 %all_to_all.35 = bf16[64,1,1,8,2,128]{5,4,3,2,1,0:T(2,128)(2,1)S(1)} all-to-all(bf16[64,1,1,8,2,128]{5,4,3,2,1,0:T(2,128)(2,1)S(1)} %stack.43), channel_id=1, replica_groups=mesh['dp'=64,'space'=8] {'dp'}, dimensions={0} | all-to-all | bytes 524288 | tf_op jit(solution)/shard_map/all_to_all | solution.py:116
  382.8 0.2 fusion.17
  383.0 0.6 copy.95
  383.6 6.4 all-to-all-start.3
  390.0 0.9 convolution_bitcast_fusion.2
  390.9 4.6 all-to-all-done.3
  395.5 0.6 copy-done.1
  396.2 95.4 %psum.15 = f32[128]{0:T(128)} all-reduce(f32[128]{0:T(128)S(1)} %get-tuple-element.28), channel_id=1, replica_groups=mesh['dp'=64,'space'=8] {'dp','space'}, use_global_device_ids=true, to_apply=%region_3.4 | all-reduce | flops 128 | bytes 1024 | tf_op jit(solution)/shard_map/psum | solution.py:69
  491.6 163.8 %all-reduce.2.cloned.1.call-done = f32[128,128]{0,1:T(8,128)} async-done(((f32[128,128]{0,1:T(8,128)}), f32[128,128]{0,1:T(8,128)}) %all-reduce.2.cloned.1.call-update) | async-done | bytes 65552 | tf_op jit(solution)/shard_map/psum | solution.py:69
  655.3 1.6 copy.98
  656.9 0.4 multiply_bitcast_fusion
  657.3 0.1 fusion.20
  657.4 1.0 fusion.18
  658.4 33.7 %all-gather.2.cloned.1.call-done = bf16[1,64,128,128]{3,2,0,1:T(8,128)(2,1)} async-done(((bf16[1,1,128,128]{3,2,0,1:T(8,128)(2,1)}), bf16[1,64,128,128]{3,2,0,1:T(8,128)(2,1)}) %all-gather.2.cloned.1.call-update) | async-done | bytes 2097168 | tf_op jit(solution)/shard_map/all_gather | solution.py:125
  692.1 2.1 fusion.13
  694.2 0.9 fusion.3
  (26 shorter events, 0.5 us)
Async XLA Ops:
  8.0 358.4 %copy-start = (bf16[1,8,2,128,128]{4,3,2,1,0:T(8,128)(2,1)S(1)}, bf16[1,8,2,128,128]{4,3,2,1,0:T(8,128)(2,1)}, u32[]{:S(2)}) copy-start(bf16[1,8,2,128,128]{4,3,2,1,0:T(8,128)(2,1)} %param.8) | copy-start | bytes 1572868
  10.9 28.2 %all-to-all-start = ((bf16[2,1,64,8,128]{4,3,1,0,2:T(8,128)(2,1)}), bf16[2,1,64,8,128]{4,3,1,0,2:T(8,128)(2,1)S(1)}, u32[]{:S(2)}, u32[]{:S(2)}) async-start(bf16[2,1,64,8,128]{4,3,1,0,2:T(8,128)(2,1)} %pad_maximum_fusion), calls=%async_computation | async-start | bytes 524288 | tf_op jit(solution)/shard_map/all_to_all | solution.py:71
  40.0 12.2 %all-to-all-start.1 = ((bf16[2,1,1,128,128]{4,0,2,1,3:T(2,128)(2,1)}), bf16[2,1,1,128,128]{4,0,2,1,3:T(2,128)(2,1)S(1)}, u32[]{:S(2)}, u32[]{:S(2)}) async-start(bf16[2,1,1,128,128]{4,0,2,1,3:T(2,128)(2,1)} %copy.85), calls=%async_computation.1 | async-start | bytes 131072 | tf_op jit(solution)/shard_map/all_to_all | solution.py:72
  46.6 319.1 %reduce-scatter.2.cloned.1.call-start = ((), (), s32[]{:S(2)}) async-start(), calls=%async_computation.5 | async-start | bytes 1064960 | tf_op jit(solution)/shard_map/reduce_scatter | solution.py:84
  52.6 337.4 %copy-start.2 = (bf16[1,64,8,128]{3,2,1,0:T(8,128)(2,1)S(1)}, bf16[1,64,8,128]{3,2,1,0:T(8,128)(2,1)}, u32[]{:S(2)}) copy-start(bf16[1,64,8,128]{3,2,1,0:T(8,128)(2,1)} %param.5) | copy-start | bytes 393220
  383.6 11.9 %all-to-all-start.3 = ((bf16[1,8,16,128]{3,2,0,1:T(8,128)(2,1)}), bf16[1,8,16,128]{3,2,0,1:T(8,128)(2,1)S(1)}, u32[]{:S(2)}, u32[]{:S(2)}) async-start(bf16[1,8,16,128]{3,2,0,1:T(8,128)(2,1)} %copy.95), calls=%async_computation.4 | async-start | bytes 65536 | tf_op jit(solution)/shard_map/all_to_all | solution.py:121
  390.0 265.3 %all-reduce.2.cloned.1.call-start = ((), (), s32[]{:S(2)}) async-start(), calls=%async_computation.7 | async-start | bytes 131072 | tf_op jit(solution)/shard_map/psum | solution.py:69
  390.9 301.2 %all-gather.2.cloned.1.call-start = ((), (), s32[]{:S(2)}) async-start(), calls=%async_computation.6 | async-start | bytes 2129920 | tf_op jit(solution)/shard_map/all_gather | solution.py:125
  395.5 0.6 copy-start.1
  657.4 36.8 %copy-start.3 = (bf16[128,128]{1,0:T(8,128)(2,1)S(1)}, bf16[128,128]{1,0:T(8,128)(2,1)}, u32[]{:S(2)}) copy-start(bf16[128,128]{1,0:T(8,128)(2,1)} %param.9) | copy-start | bytes 98308
Sparse Core Ops, SparseCore 0:
  54.4 311.3 reduce-scatter.1
  396.3 295.7 all-gather.1
Sparse Core Ops, SparseCore 1:
  396.8 258.5 all-reduce.1
